TPU v7x, 32 devices: a whole 2x2x4 slice. The times are simulated.
32 devices in a mesh: expert: 4 (over z), tensor: 8 (over y, x, core).
Axes of the slice: x: 2, y: 2, z: 4, core: 2. Of those that a mesh axis runs over, the one named last changes fastest.
Arguments:
- activations: bfloat16 [3072, 512], P('tensor', 'expert'), may hold values from -6 to 6
- cotangent: bfloat16 [3072, 512], P('tensor', 'expert'), may hold values from -4 to 4
- route_ids: int32 [512, 2], P('expert'), may hold values from 0 to 3, all different within a row; in each aligned block of 128 rows (0 to 127, 128 to 255, ...) at most 80 rows name the same one
- gate_probs: float32 [512, 2], P('expert'), may hold values from 0.2 to 0.8
- gate_weight: bfloat16 [4, 3072, 16384], P('expert', None, 'tensor'), may hold values from -0.15625 to 0.15625
- up_weight: bfloat16 [4, 3072, 16384], P('expert', None, 'tensor'), may hold values from -0.15625 to 0.15625
- down_weight: bfloat16 [4, 16384, 3072], P('expert', 'tensor'), may hold values from -0.046875 to 0.046875
Outputs:
- grad_input: bfloat16 [3072, 512], P('tensor', 'expert')
- score_grad: float32 [512, 2], P('expert')
Inputs may be any that keep to these rules, and one draw needn't show every extreme that they name: `route_ids`: each token names 2 different experts. Among the 128 tokens of one index of the expert axis no expert is named more than 80 times, and in every draw some such block names one expert exactly 80 times.
All inputs are finite; a program needn't handle non-finite values.
Results may differ from a plain program's by a relative error of at most 0.008.
Values may be sent and summed in bfloat16 or wider, within the bound.
A program may use at most 128 MiB of HBM per device.

v0:
```python
import jax
import jax.numpy as jnp
from jax import lax
from jax.sharding import PartitionSpec as P

EXTRA_ROWS = 16


def slot_numbers(route_ids, expert_count, capacity):
    token_count = route_ids.shape[0]
    onehot = route_ids[:, :, None] == jnp.arange(expert_count, dtype=jnp.int32)[None, None, :]
    named = jnp.sum(onehot.astype(jnp.float32), axis=1).astype(jnp.bfloat16)
    order = jnp.arange(token_count, dtype=jnp.int32)
    before = (order[None, :] < order[:, None]).astype(jnp.bfloat16)
    earlier = jnp.dot(before, named, preferred_element_type=jnp.float32)
    position = jnp.sum(jnp.where(onehot, earlier[:, None, :], 0.0), axis=2).astype(jnp.int32)
    return route_ids * capacity + position


def swiglu_backward(gate_sum, up_sum, hidden_grad):
    sigma = jax.nn.sigmoid(gate_sum)
    silu_value = gate_sum * sigma
    grad_up = (hidden_grad * silu_value).astype(jnp.bfloat16)
    grad_gate = (hidden_grad * up_sum * sigma * (1.0 + gate_sum * (1.0 - sigma))).astype(
        jnp.bfloat16
    )
    score_rows = jnp.sum(silu_value * up_sum * hidden_grad, axis=1)
    return (grad_gate, grad_up, score_rows)


def body(activations, cotangent, route_ids, gate_probs, gate_weight, up_weight, down_weight):
    expert_count = lax.axis_size("expert")
    tokens_here = route_ids.shape[0]
    capacity = min(tokens_here, 5 * tokens_here // (2 * expert_count))
    slot_total = expert_count * capacity
    destination = slot_numbers(route_ids, expert_count, capacity)
    slot_range = jnp.arange(slot_total, dtype=jnp.int32)
    matches = destination[:, :, None] == slot_range[None, None, :]
    placing = jnp.sum(matches.astype(jnp.float32), axis=1).astype(jnp.bfloat16)
    weighting = jnp.sum(jnp.where(matches, gate_probs[:, :, None], jnp.float32(0.0)), axis=1)
    gate_local = gate_weight[0]
    up_local = up_weight[0]
    down_local = down_weight[0]
    first_dims = (((0,), (0,)), ((), ()))
    down_dims = (((0,), (1,)), ((), ()))
    hidden_dims = (((1,), (1,)), ((), ()))
    features_here = activations.shape[0]
    send_in = jnp.dot(activations, placing, preferred_element_type=jnp.float32).astype(jnp.bfloat16)
    send_grad = jnp.dot(cotangent, placing, preferred_element_type=jnp.float32).astype(jnp.bfloat16)
    recv_in, recv_grad = (
        lax.all_to_all(send_in, "expert", split_axis=1, concat_axis=1, tiled=True),
        lax.all_to_all(send_grad, "expert", split_axis=1, concat_axis=1, tiled=True),
    )
    feature_piece = lax.all_gather(recv_in, "tensor", axis=0, tiled=True)
    grad_piece = lax.all_gather(recv_grad, "tensor", axis=0, tiled=True)
    gate_rows = gate_local
    up_rows = up_local
    gate_sum = lax.dot_general(
        feature_piece, gate_rows, first_dims, preferred_element_type=jnp.float32
    )
    up_sum = lax.dot_general(feature_piece, up_rows, first_dims, preferred_element_type=jnp.float32)
    hidden_grad = lax.dot_general(
        grad_piece, down_local, down_dims, preferred_element_type=jnp.float32
    )
    gate_sum, up_sum, hidden_grad = (gate_sum, up_sum, hidden_grad)
    grad_gate, grad_up, score_rows = swiglu_backward(gate_sum, up_sum, hidden_grad)
    gate_rows = gate_local
    up_rows = up_local
    term = lax.dot_general(gate_rows, grad_gate, hidden_dims, preferred_element_type=jnp.float32)
    term = term + lax.dot_general(up_rows, grad_up, hidden_dims, preferred_element_type=jnp.float32)
    tensor_count = lax.axis_size("tensor")
    score_high = score_rows.astype(jnp.bfloat16)
    score_low = (score_rows - score_high.astype(jnp.float32)).astype(jnp.bfloat16)
    extra = jnp.concatenate(
        [
            score_high[None, :],
            score_low[None, :],
            jnp.zeros((EXTRA_ROWS - 2, slot_total), jnp.bfloat16),
        ],
        axis=0,
    )
    blocks = term.astype(jnp.bfloat16).reshape(tensor_count, features_here, slot_total)
    extra = jnp.broadcast_to(extra[None], (tensor_count, EXTRA_ROWS, slot_total))
    parts = lax.all_to_all(
        jnp.concatenate([blocks, extra], axis=1), "tensor", split_axis=0, concat_axis=0, tiled=True
    ).astype(jnp.float32)
    totals = jnp.sum(parts, axis=0)
    score = (
        totals[features_here : features_here + 1] + totals[features_here + 1 : features_here + 2]
    )
    score_high = score.astype(jnp.bfloat16)
    score_low = (score - score_high.astype(jnp.float32)).astype(jnp.bfloat16)
    summed = jnp.concatenate(
        [
            totals[:features_here].astype(jnp.bfloat16),
            score_high,
            score_low,
            jnp.zeros((EXTRA_ROWS - 2, slot_total), jnp.bfloat16),
        ],
        axis=0,
    )
    back = lax.all_to_all(summed, "expert", split_axis=1, concat_axis=1, tiled=True)
    back = back.astype(jnp.float32)
    back_terms = back[:features_here]
    back_scores = (
        back[features_here : features_here + 1] + back[features_here + 1 : features_here + 2]
    )
    grad_local = jnp.dot(
        back_terms, weighting.T, precision=lax.Precision.HIGHEST, preferred_element_type=jnp.float32
    )
    score_grad = jnp.sum(
        jnp.where(matches, back_scores[0][None, None, :], jnp.float32(0.0)), axis=2
    )
    grad_input = grad_local.astype(jnp.bfloat16)
    return (grad_input, score_grad)


def solution(mesh):
    in_specs = (
        P("tensor", "expert"),
        P("tensor", "expert"),
        P("expert", None),
        P("expert", None),
        P("expert", None, "tensor"),
        P("expert", None, "tensor"),
        P("expert", "tensor", None),
    )
    out_specs = (P("tensor", "expert"), P("expert", None))
    return jax.shard_map(body, mesh=mesh, in_specs=in_specs, out_specs=out_specs, check_vma=False)
```

profile of v0, /device:TPU:0, one launch (start us, length us, event | category | flops | bytes accessed | tf_op | source)
XLA Modules:
  0.0 178.5 jit_solution(15263084820237573660)
XLA Ops:
  7.2 0.0 copy-start
  7.2 0.0 all-gather.5.cloned.1.call-start
  7.2 0.7 convert_reduce_fusion.2
  7.9 0.1 fusion.23
  8.1 0.7 select_reduce_fusion.2
  8.8 0.7 convert_add_fusion
  9.5 0.0 copy-done
  9.5 0.2 convolution_convert_fusion
  9.8 14.7 %all_to_all.38 = bf16[384,4,80]{0,2,1:T(8,128)(2,1)} all-to-all(bf16[384,4,80]{0,2,1:T(8,128)(2,1)S(1)} %bitcast.50), channel_id=1, replica_groups=mesh['expert'=4,'tensor'=8] {'expert'}, dimensions={1} | all-to-all | bytes 491520 | tf_op jit(solution)/shard_map/all_to_all | solution.py:51
  24.5 0.0 all-gather.5.cloned.1.call-update
  24.5 0.0 all-gather.3.cloned.1.call-start
  24.6 1.1 convolution_convert_fusion.1
  25.7 10.7 %all_to_all.39 = bf16[384,4,80]{0,2,1:T(8,128)(2,1)} all-to-all(bf16[384,4,80]{0,2,1:T(8,128)(2,1)S(1)} %bitcast.49), channel_id=1, replica_groups=mesh['expert'=4,'tensor'=8] {'expert'}, dimensions={1} | all-to-all | bytes 491520 | tf_op jit(solution)/shard_map/all_to_all | solution.py:52
  36.5 0.0 all-gather.3.cloned.1.call-update
  36.5 14.9 %all-gather.5.cloned.1.call-done = bf16[3072,320]{0,1:T(8,128)(2,1)} async-done(((bf16[384,320]{0,1:T(8,128)(2,1)}), bf16[3072,320]{0,1:T(8,128)(2,1)}) %all-gather.5.cloned.1.call-update) | async-done | bytes 1966096 | tf_op jit(solution)/shard_map/all_gather | solution.py:54
  51.4 0.0 copy-start.3
  51.4 9.4 %fusion.2 = f32[320,2048]{1,0:T(8,128)S(1)} fusion(bf16[3072,320]{0,1:T(8,128)(2,1)} %all-gather.5.cloned.1.call-done, bf16[1,3072,2048]{2,1,0:T(8,128)(2,1)} %param.11), kind=kOutput, calls=%fused_computation.2 | convolution fusion | flops 4026531840 | bytes 17170432 | tf_op jit(solution)/shard_map/dot_general | solution.py:58
  60.8 0.0 copy-done.3
  60.8 8.8 %fusion.6 = f32[320,2048]{1,0:T(8,128)} fusion(bf16[3072,320]{0,1:T(8,128)(2,1)S(1)} %copy-done.3, bf16[1,3072,2048]{2,1,0:T(8,128)(2,1)} %param.12), kind=kOutput, calls=%fused_computation.6 | convolution fusion | flops 4026531840 | bytes 17170432 | tf_op jit(solution)/shard_map/dot_general | solution.py:61
  69.6 11.3 %all-gather.3.cloned.1.call-done = bf16[3072,320]{0,1:T(8,128)(2,1)} async-done(((bf16[384,320]{0,1:T(8,128)(2,1)}), bf16[3072,320]{0,1:T(8,128)(2,1)}) %all-gather.3.cloned.1.call-update) | async-done | bytes 1966096 | tf_op jit(solution)/shard_map/all_gather | solution.py:55
  80.9 12.0 %multiply_reduce_fusion = (f32[320]{0:T(512)S(1)}, f32[320,2048]{1,0:T(8,128)}) fusion(f32[320,2048]{1,0:T(8,128)} %fusion.6, f32[320,2048]{1,0:T(8,128)S(1)} %fusion.2, bf16[3072,320]{0,1:T(8,128)(2,1)} %all-gather.3.cloned.1.call-done, bf16[1,2048,3072]{2,1,0:T(8,128)(2,1)} %param.13), kind=kOutput, calls=%fused_computation.14 | convolution fusion | flops 4031119104 | bytes 22414592 | tf_op jit(solution)/shard_map/dot_general | solution.py:62
  93.0 12.8 %fusion = f32[320,3072]{1,0:T(8,128)} fusion(bf16[1,3072,2048]{2,1,0:T(8,128)(2,1)} %param.11, f32[320,2048]{1,0:T(8,128)S(1)} %fusion.2, f32[320,2048]{1,0:T(8,128)} %get-tuple-element.7, f32[320,2048]{1,0:T(8,128)} %fusion.6), kind=kOutput, calls=%fused_computation | convolution fusion | flops 4033085440 | bytes 24379392 | tf_op jit(solution)/shard_map/dot_general | solution.py:69
  105.8 12.1 %fusion.16 = bf16[3072,320]{0,1:T(8,128)(2,1)} fusion(f32[320,3072]{1,0:T(8,128)} %fusion, bf16[1,3072,2048]{2,1,0:T(8,128)(2,1)} %param.12, f32[320,2048]{1,0:T(8,128)} %get-tuple-element.7, f32[320,2048]{1,0:T(8,128)S(1)} %fusion.2), kind=kOutput, calls=%fused_computation.13 | convolution fusion | flops 4032430080 | bytes 23724032 | tf_op jit(solution)/shard_map/dot_general | solution.py:70
  117.9 2.9 %copy.40 = bf16[3072,320]{1,0:T(8,128)(2,1)S(1)} copy(bf16[3072,320]{0,1:T(8,128)(2,1)} %fusion.16) | data formatting | bytes 3932160 | tf_op jit(solution)/shard_map/reshape | solution.py:82
  120.9 0.3 pad_maximum_fusion
  121.1 33.0 %all_to_all.40 = bf16[8,400,320]{2,1,0:T(8,128)(2,1)S(1)} all-to-all(bf16[8,400,320]{2,1,0:T(8,128)(2,1)S(1)} %pad_maximum_fusion), channel_id=1, replica_groups=mesh['expert'=4,'tensor'=8] {'tensor'}, dimensions={0} | all-to-all | bytes 4096000 | tf_op jit(solution)/shard_map/all_to_all | solution.py:84
  154.1 0.0 copy-start.1
  154.1 0.4 convert_reduce_fusion
  154.5 0.0 copy-start.2
  154.7 0.2 copy.39
  154.8 14.5 %all_to_all.41 = bf16[400,4,80]{0,2,1:T(8,128)(2,1)S(1)} all-to-all(bf16[400,4,80]{0,2,1:T(8,128)(2,1)S(1)} %bitcast.45), channel_id=1, replica_groups=mesh['expert'=4,'tensor'=8] {'expert'}, dimensions={1} | all-to-all | bytes 512000 | tf_op jit(solution)/shard_map/all_to_all | solution.py:102
  169.3 0.1 convert_element_type.115
  169.4 0.2 fusion.22
  169.6 0.1 broadcast_in_dim.57
  169.7 0.0 copy-done.2
  169.7 0.7 select_reduce_fusion
  170.4 1.2 convolution_convert_fusion.2
  171.6 0.0 copy-done.1
  (10 shorter events, 0.2 us)
Async XLA Ops:
  7.2 2.3 %copy-start = (bf16[384,128]{1,0:T(8,128)(2,1)S(1)}, bf16[384,128]{1,0:T(8,128)(2,1)}, u32[]{:S(2)}) copy-start(bf16[384,128]{1,0:T(8,128)(2,1)} %param.7) | copy-start | bytes 294916
  7.2 44.2 %all-gather.5.cloned.1.call-start = ((), (), s32[]{:S(2)}) async-start(), calls=%async_computation.5 | async-start | bytes 2211840 | tf_op jit(solution)/shard_map/all_gather | solution.py:54
  24.5 56.4 %all-gather.3.cloned.1.call-start = ((), (), s32[]{:S(2)}) async-start(), calls=%async_computation.4 | async-start | bytes 2211840 | tf_op jit(solution)/shard_map/all_gather | solution.py:55
  51.4 9.4 %copy-start.3 = (bf16[3072,320]{0,1:T(8,128)(2,1)S(1)}, bf16[3072,320]{0,1:T(8,128)(2,1)}, u32[]{:S(2)}) copy-start(bf16[3072,320]{0,1:T(8,128)(2,1)} %all-gather.5.cloned.1.call-done) | copy-start | bytes 5898244
  154.1 17.5 %copy-start.1 = (bf16[384,128]{1,0:T(8,128)(2,1)S(1)}, bf16[384,128]{1,0:T(8,128)(2,1)}, u32[]{:S(2)}) copy-start(bf16[384,128]{1,0:T(8,128)(2,1)} %param.7) | copy-start | bytes 294916
  154.5 15.2 %copy-start.2 = (f32[128,2]{0,1:T(2,128)S(1)}, f32[128,2]{0,1:T(2,128)}, u32[]{:S(2)}) copy-start(f32[128,2]{0,1:T(2,128)} %param.10) | copy-start | bytes 3076
Sparse Core Ops, SparseCore 0:
  24.7 26.7 all-gather.4
  53.3 27.6 all-gather.2
where the time goes:
time: 179 us; the launch traced here: 178 us
  blocking collectives  73 us (41%)
  matrix products  57.8 us (32%)
  waiting for transfers between devices  26.3 us (15%)
  between operations  14.2 us (8%)
  other arithmetic  3.87 us (2%)
  local copies, waits for them, and re-layouts  3.26 us (2%)
    all_to_all x1, blocking collectives, body(): lax.all_to_all(jnp.concatenate([blocks, extra], axis=1), 'tensor', split_...  33 us
    all_gather x1, waiting for transfers between devices, body(): feature_piece = lax.all_gather(recv_in, 'tensor', axis=0, tiled=True)  14.9 us
    all_to_all x1, blocking collectives, body(): lax.all_to_all(send_in, 'expert', split_axis=1, concat_axis=1, tiled=True)  14.7 us
    all_to_all x1, blocking collectives, body(): lax.all_to_all(summed, 'expert', split_axis=1, concat_axis=1, tiled=True)  14.5 us
    dot_general x1, matrix products, body(): lax.dot_general(gate_rows, grad_gate, hidden_dims, preferred_element_type...  12.8 us
    dot_general x1, matrix products, body(): lax.dot_general(up_rows, grad_up, hidden_dims, preferred_element_type=jnp...  12.1 us
    dot_general x1, matrix products, body(): lax.dot_general(grad_piece, down_local, down_dims, preferred_element_type...  12 us
    all_gather x1, waiting for transfers between devices, body(): grad_piece = lax.all_gather(recv_grad, 'tensor', axis=0, tiled=True)  11.3 us
  transfers between devices with their start and end apart: 2, of which 2 were waited for; matrix products, arithmetic and copies ran while one was open for 11% of the time, Pallas kernels for 0%

commit v1 on v0

--- a/solution.py
+++ b/solution.py
@@ -52,7 +52,14 @@
         lax.all_to_all(send_grad, "expert", split_axis=1, concat_axis=1, tiled=True),
     )
     feature_piece = lax.all_gather(recv_in, "tensor", axis=0, tiled=True)
-    grad_piece = lax.all_gather(recv_grad, "tensor", axis=0, tiled=True)
+    ring = [recv_grad]
+    for hop in range(7):
+        ring.append(lax.ppermute(ring[-1], "tensor", [(dev, (dev + 1) % 8) for dev in range(8)]))
+    grad_piece = jnp.roll(
+        jnp.concatenate(ring[::-1], axis=0),
+        (lax.axis_index("tensor") + 1) * ring[0].shape[0],
+        axis=0,
+    )
     gate_rows = gate_local
     up_rows = up_local
     gate_sum = lax.dot_general(

time: 179 us -> 207 us (1.16)
  waiting for transfers between devices: 26.3 us -> 56.6 us
  blocking collectives: 73 us -> 47.5 us
  local copies, waits for them, and re-layouts: 3.26 us -> 16.2 us
  starting transfers between devices: 0.08 us -> 9.88 us
    ppermute x0 -> x7, waiting for transfers between devices: none -> 43.2 us  [body(): lax.ppermute(ring[-1], 'tensor', [(dev, (dev + 1) % 8) for dev in range(8)])]
    all_to_all x2 -> x0, blocking collectives: 25.5 us -> none  [the longest x1 14.7 us: body(): lax.all_to_all(send_in, 'expert', split_axis=1, concat_axis=1, tiled=True)]
    all_gather x1, waiting for transfers between devices: 14.9 us -> 0.01 us  [body(): feature_piece = lax.all_gather(recv_in, 'tensor', axis=0, tiled=True)]
    all_to_all x0 -> x2, waiting for transfers between devices: none -> 13.3 us  [the longest x1 6.75 us: body(): lax.all_to_all(send_grad, 'expert', split_axis=1, concat_axis=1, tiled=True)]
    unnamed x8 -> x27, local copies, waits for them, and re-layouts: 0.03 us -> 12.2 us
    all_gather x1 -> x0, waiting for transfers between devices: 11.3 us -> none  [body(): grad_piece = lax.all_gather(recv_grad, 'tensor', axis=0, tiled=True)]
    all_to_all x0 -> x2, starting transfers between devices: none -> 9.71 us  [the longest x1 6.31 us: body(): lax.all_to_all(send_grad, 'expert', split_axis=1, concat_axis=1, tiled=True)]
  transfers between devices with their start and end apart: 2 -> 10, of which waited for: 2 -> 8; matrix products, arithmetic and copies ran while one was open for 11% -> 7% of each run, Pallas kernels for 0% -> 0%
where the time goes in v1:
time: 207 us
  matrix products  58.3 us (28%)
  waiting for transfers between devices  56.6 us (27%)
  blocking collectives  47.5 us (23%)
  local copies, waits for them, and re-layouts  16.2 us (8%)
  between operations  14.2 us (7%)
  starting transfers between devices  9.88 us (5%)
  other arithmetic  3.9 us (2%)
    ppermute x7, waiting for transfers between devices, body(): lax.ppermute(ring[-1], 'tensor', [(dev, (dev + 1) % 8) for dev in range(8)])  43.2 us
    all_to_all x1, blocking collectives, body(): lax.all_to_all(jnp.concatenate([blocks, extra], axis=1), 'tensor', split_...  33 us
    all_to_all x1, blocking collectives, body(): lax.all_to_all(summed, 'expert', split_axis=1, concat_axis=1, tiled=True)  14.5 us
    dot_general x1, matrix products, body(): lax.dot_general(gate_rows, grad_gate, hidden_dims, preferred_element_type...  12.8 us
    dot_general x1, matrix products, body(): lax.dot_general(grad_piece, down_local, down_dims, preferred_element_type...  12.3 us
    dot_general x1, matrix products, body(): lax.dot_general(up_rows, grad_up, hidden_dims, preferred_element_type=jnp...  12.3 us
    unnamed x27, local copies, waits for them, and re-layouts  12.2 us
    dot_general x1, matrix products, body(): lax.dot_general(feature_piece, gate_rows, first_dims, preferred_element_t...  9.42 us
  transfers between devices with their start and end apart: 10, of which 8 were waited for; matrix products, arithmetic and copies ran while one was open for 7% of the time, Pallas kernels for 0%

profile of v1, /device:TPU:0, one launch (start us, length us, event | category | flops | bytes accessed | tf_op | source)
XLA Modules:
  0.0 206.6 jit_solution(17757942513348049886)
XLA Ops:
  7.2 0.7 convert_reduce_fusion.2
  7.9 0.1 fusion.24
  8.0 0.7 select_reduce_fusion.2
  8.8 0.7 convert_add_fusion
  9.5 0.9 convolution_convert_fusion.1
  10.4 6.3 %all-to-all-start = ((bf16[384,4,80]{0,2,1:T(8,128)(2,1)}), bf16[384,4,80]{0,2,1:T(8,128)(2,1)S(1)}, u32[]{:S(2)}, u32[]{:S(2)}) async-start(bf16[384,4,80]{0,2,1:T(8,128)(2,1)} %bitcast.1), calls=%async_computation | async-start | bytes 491520 | tf_op jit(solution)/shard_map/all_to_all | solution.py:52
  16.7 1.8 convolution_convert_fusion
  18.6 6.8 %all-to-all-done = bf16[384,4,80]{0,2,1:T(8,128)(2,1)S(1)} async-done(((bf16[384,4,80]{0,2,1:T(8,128)(2,1)}), bf16[384,4,80]{0,2,1:T(8,128)(2,1)S(1)}, u32[]{:S(2)}, u32[]{:S(2)}) %all-to-all-start) | async-done | bytes 245792 | tf_op jit(solution)/shard_map/all_to_all | solution.py:52
  25.3 3.4 %all-to-all-start.1 = ((bf16[384,4,80]{0,2,1:T(8,128)(2,1)}), bf16[384,4,80]{0,2,1:T(8,128)(2,1)S(1)}, u32[]{:S(2)}, u32[]{:S(2)}) async-start(bf16[384,4,80]{0,2,1:T(8,128)(2,1)} %bitcast.5), calls=%async_computation.1 | async-start | bytes 491520 | tf_op jit(solution)/shard_map/all_to_all | solution.py:51
  28.8 6.5 %all-to-all-done.1 = bf16[384,4,80]{0,2,1:T(8,128)(2,1)S(1)} async-done(((bf16[384,4,80]{0,2,1:T(8,128)(2,1)}), bf16[384,4,80]{0,2,1:T(8,128)(2,1)S(1)}, u32[]{:S(2)}, u32[]{:S(2)}) %all-to-all-start.1) | async-done | bytes 245792 | tf_op jit(solution)/shard_map/all_to_all | solution.py:51
  35.4 0.7 copy-done.2
  36.2 6.5 %collective-permute-done.1 = bf16[384,320]{0,1:T(8,128)(2,1)S(1)} collective-permute-done((bf16[384,320]{0,1:T(8,128)(2,1)S(1)}, bf16[384,320]{0,1:T(8,128)(2,1)S(1)}, u32[]{:S(2)}, u32[]{:S(2)}) %collective-permute-start.1) | collective-permute-done | bytes 245792 | tf_op jit(solution)/shard_map/ppermute | solution.py:57
  42.7 9.2 %collective-permute-done.2 = bf16[384,320]{0,1:T(8,128)(2,1)S(1)} collective-permute-done((bf16[384,320]{0,1:T(8,128)(2,1)S(1)}, bf16[384,320]{0,1:T(8,128)(2,1)S(1)}, u32[]{:S(2)}, u32[]{:S(2)}) %collective-permute-start.2) | collective-permute-done | bytes 245792 | tf_op jit(solution)/shard_map/ppermute | solution.py:57
  51.8 6.6 %collective-permute-done.3 = bf16[384,320]{0,1:T(8,128)(2,1)S(1)} collective-permute-done((bf16[384,320]{0,1:T(8,128)(2,1)S(1)}, bf16[384,320]{0,1:T(8,128)(2,1)S(1)}, u32[]{:S(2)}, u32[]{:S(2)}) %collective-permute-start.3) | collective-permute-done | bytes 245792 | tf_op jit(solution)/shard_map/ppermute | solution.py:57
  58.4 7.9 %collective-permute-done.4 = bf16[384,320]{0,1:T(8,128)(2,1)S(1)} collective-permute-done((bf16[384,320]{0,1:T(8,128)(2,1)S(1)}, bf16[384,320]{0,1:T(8,128)(2,1)S(1)}, u32[]{:S(2)}, u32[]{:S(2)}) %collective-permute-start.4) | collective-permute-done | bytes 245792 | tf_op jit(solution)/shard_map/ppermute | solution.py:57
  66.4 6.5 %collective-permute-done.5 = bf16[384,320]{0,1:T(8,128)(2,1)S(1)} collective-permute-done((bf16[384,320]{0,1:T(8,128)(2,1)S(1)}, bf16[384,320]{0,1:T(8,128)(2,1)S(1)}, u32[]{:S(2)}, u32[]{:S(2)}) %collective-permute-start.5) | collective-permute-done | bytes 245792 | tf_op jit(solution)/shard_map/ppermute | solution.py:57
  72.9 6.5 %collective-permute-done.6 = bf16[384,320]{0,1:T(8,128)(2,1)S(1)} collective-permute-done((bf16[384,320]{0,1:T(8,128)(2,1)S(1)}, bf16[384,320]{0,1:T(8,128)(2,1)S(1)}, u32[]{:S(2)}, u32[]{:S(2)}) %collective-permute-start.6) | collective-permute-done | bytes 245792 | tf_op jit(solution)/shard_map/ppermute | solution.py:57
  79.4 0.8 constant_dynamic-update-slice_fusion.15
  80.2 0.8 constant_dynamic-update-slice_fusion.14
  81.0 0.7 constant_dynamic-update-slice_fusion.13
  81.7 0.7 constant_dynamic-update-slice_fusion.12
  82.4 0.8 constant_dynamic-update-slice_fusion.11
  83.2 0.8 constant_dynamic-update-slice_fusion.10
  84.0 0.8 constant_dynamic-update-slice_fusion.9
  84.8 0.8 constant_dynamic-update-slice_fusion.8
  85.6 0.8 constant_dynamic-update-slice_fusion.7
  86.4 0.8 constant_dynamic-update-slice_fusion.6
  87.1 0.8 constant_dynamic-update-slice_fusion.5
  87.9 0.8 constant_dynamic-update-slice_fusion.4
  88.6 0.8 constant_dynamic-update-slice_fusion.3
  89.4 0.8 constant_dynamic-update-slice_fusion.2
  90.2 0.8 constant_dynamic-update-slice_fusion.1
  90.9 0.8 constant_dynamic-update-slice_fusion
  91.7 9.4 %fusion.2 = f32[320,2048]{1,0:T(8,128)S(1)} fusion(bf16[3072,320]{0,1:T(8,128)(2,1)} %all-gather.2.cloned.1.call-done, bf16[1,3072,2048]{2,1,0:T(8,128)(2,1)} %param.11), kind=kOutput, calls=%fused_computation.2 | convolution fusion | flops 4026531840 | bytes 17170432 | tf_op jit(solution)/shard_map/dot_general | solution.py:65
  101.1 7.4 %fusion.6 = f32[320,2048]{1,0:T(8,128)S(1)} fusion(bf16[3072,320]{0,1:T(8,128)(2,1)S(1)} %copy-done.4, bf16[1,3072,2048]{2,1,0:T(8,128)(2,1)} %param.12), kind=kOutput, calls=%fused_computation.6 | convolution fusion | flops 4026531840 | bytes 17170432 | tf_op jit(solution)/shard_map/dot_general | solution.py:68
  108.5 12.3 %multiply_reduce_fusion = (f32[320]{0:T(512)S(1)}, f32[320,2048]{1,0:T(8,128)}) fusion(f32[320,2048]{1,0:T(8,128)S(1)} %fusion.6, f32[320,2048]{1,0:T(8,128)S(1)} %fusion.2, bf16[1,2048,3072]{2,1,0:T(8,128)(2,1)} %param.13, bf16[6144,320]{0,1:T(8,128)(2,1)} %constant_dynamic-update-slice_fusion, s32[]{:T(128)S(6)} %select_n.27), kind=kOutput, calls=%fused_computation.14 | convolution fusion | flops 4031119104 | bytes 22414596 | tf_op jit(solution)/shard_map/dot_general | solution.py:69
  120.9 12.8 %fusion = f32[320,3072]{1,0:T(8,128)} fusion(bf16[1,3072,2048]{2,1,0:T(8,128)(2,1)} %param.11, f32[320,2048]{1,0:T(8,128)S(1)} %fusion.2, f32[320,2048]{1,0:T(8,128)} %get-tuple-element.7, f32[320,2048]{1,0:T(8,128)} %copy-done.5), kind=kOutput, calls=%fused_computation | convolution fusion | flops 4033085440 | bytes 24379392 | tf_op jit(solution)/shard_map/dot_general | solution.py:76
  133.7 12.3 %fusion.16 = bf16[3072,320]{0,1:T(8,128)(2,1)} fusion(f32[320,3072]{1,0:T(8,128)} %fusion, bf16[1,3072,2048]{2,1,0:T(8,128)(2,1)} %param.12, f32[320,2048]{1,0:T(8,128)} %get-tuple-element.7, f32[320,2048]{1,0:T(8,128)S(1)} %fusion.2), kind=kOutput, calls=%fused_computation.13 | convolution fusion | flops 4032430080 | bytes 23724032 | tf_op jit(solution)/shard_map/dot_general | solution.py:77
  146.0 2.9 %copy.40 = bf16[3072,320]{1,0:T(8,128)(2,1)S(1)} copy(bf16[3072,320]{0,1:T(8,128)(2,1)} %fusion.16) | data formatting | bytes 3932160 | tf_op jit(solution)/shard_map/reshape | solution.py:89
  149.0 0.3 pad_maximum_fusion
  149.3 33.0 %all_to_all.38 = bf16[8,400,320]{2,1,0:T(8,128)(2,1)S(1)} all-to-all(bf16[8,400,320]{2,1,0:T(8,128)(2,1)S(1)} %pad_maximum_fusion), channel_id=1, replica_groups=mesh['expert'=4,'tensor'=8] {'tensor'}, dimensions={0} | all-to-all | bytes 4096000 | tf_op jit(solution)/shard_map/all_to_all | solution.py:91
  182.3 0.4 convert_reduce_fusion
  182.8 0.2 copy.39
  183.0 14.5 %all_to_all.39 = bf16[400,4,80]{0,2,1:T(8,128)(2,1)S(1)} all-to-all(bf16[400,4,80]{0,2,1:T(8,128)(2,1)S(1)} %bitcast.47), channel_id=1, replica_groups=mesh['expert'=4,'tensor'=8] {'expert'}, dimensions={1} | all-to-all | bytes 512000 | tf_op jit(solution)/shard_map/all_to_all | solution.py:109
  197.5 0.2 fusion.23
  197.8 0.1 broadcast_in_dim.57
  197.9 0.7 select_reduce_fusion
  198.6 1.2 convolution_convert_fusion.2
  (33 shorter events, 0.5 us)
Async XLA Ops:
  7.2 2.3 %copy-start = (bf16[384,128]{1,0:T(8,128)(2,1)S(1)}, bf16[384,128]{1,0:T(8,128)(2,1)}, u32[]{:S(2)}) copy-start(bf16[384,128]{1,0:T(8,128)(2,1)} %param.8) | copy-start | bytes 294916
  10.4 14.9 %all-to-all-start = ((bf16[384,4,80]{0,2,1:T(8,128)(2,1)}), bf16[384,4,80]{0,2,1:T(8,128)(2,1)S(1)}, u32[]{:S(2)}, u32[]{:S(2)}) async-start(bf16[384,4,80]{0,2,1:T(8,128)(2,1)} %bitcast.1), calls=%async_computation | async-start | bytes 491520 | tf_op jit(solution)/shard_map/all_to_all | solution.py:52
  25.3 10.1 %all-to-all-start.1 = ((bf16[384,4,80]{0,2,1:T(8,128)(2,1)}), bf16[384,4,80]{0,2,1:T(8,128)(2,1)S(1)}, u32[]{:S(2)}, u32[]{:S(2)}) async-start(bf16[384,4,80]{0,2,1:T(8,128)(2,1)} %bitcast.5), calls=%async_computation.1 | async-start | bytes 491520 | tf_op jit(solution)/shard_map/all_to_all | solution.py:51
  28.7 63.0 %all-gather.2.cloned.1.call-start = ((), (), s32[]{:S(2)}) async-start(), calls=%async_computation.4 | async-start | bytes 2211840 | tf_op jit(solution)/shard_map/all_gather | solution.py:54
  28.8 7.3 %collective-permute-start = (bf16[384,320]{0,1:T(8,128)(2,1)S(1)}, bf16[384,320]{0,1:T(8,128)(2,1)S(1)}, u32[]{:S(2)}, u32[]{:S(2)}) collective-permute-start(bf16[384,320]{0,1:T(8,128)(2,1)S(1)} %bitcast.44), channel_id=1, source_target_pairs={{0,1},{1,2},{2,3},{3,4},{4,5},{5,6},{6,7},{7,0},{8,9},{9,10},{10,1... | collective-permute-start | bytes 737288 | tf_op jit(solution)/shard_map/ppermute | solution.py:57
  35.4 0.7 copy-start.2
  36.1 6.6 %collective-permute-start.1 = (bf16[384,320]{0,1:T(8,128)(2,1)S(1)}, bf16[384,320]{0,1:T(8,128)(2,1)S(1)}, u32[]{:S(2)}, u32[]{:S(2)}) collective-permute-start(bf16[384,320]{0,1:T(8,128)(2,1)S(1)} %collective-permute-done), channel_id=1, source_target_pairs={{0,1},{1,2},{2,3},{3,4},{4,5},{5,6},{6,7},{7,0},{8,9},{9,10},{10,1... | collective-permute-start | bytes 737288 | tf_op jit(solution)/shard_map/ppermute | solution.py:57
  42.7 9.2 %collective-permute-start.2 = (bf16[384,320]{0,1:T(8,128)(2,1)S(1)}, bf16[384,320]{0,1:T(8,128)(2,1)S(1)}, u32[]{:S(2)}, u32[]{:S(2)}) collective-permute-start(bf16[384,320]{0,1:T(8,128)(2,1)S(1)} %collective-permute-done.1), channel_id=1, source_target_pairs={{0,1},{1,2},{2,3},{3,4},{4,5},{5,6},{6,7},{7,0},{8,9},{9,10},{10,1... | collective-permute-start | bytes 737288 | tf_op jit(solution)/shard_map/ppermute | solution.py:57
  51.8 6.6 %collective-permute-start.3 = (bf16[384,320]{0,1:T(8,128)(2,1)S(1)}, bf16[384,320]{0,1:T(8,128)(2,1)S(1)}, u32[]{:S(2)}, u32[]{:S(2)}) collective-permute-start(bf16[384,320]{0,1:T(8,128)(2,1)S(1)} %collective-permute-done.2), channel_id=1, source_target_pairs={{0,1},{1,2},{2,3},{3,4},{4,5},{5,6},{6,7},{7,0},{8,9},{9,10},{10,1... | collective-permute-start | bytes 737288 | tf_op jit(solution)/shard_map/ppermute | solution.py:57
  58.4 7.9 %collective-permute-start.4 = (bf16[384,320]{0,1:T(8,128)(2,1)S(1)}, bf16[384,320]{0,1:T(8,128)(2,1)S(1)}, u32[]{:S(2)}, u32[]{:S(2)}) collective-permute-start(bf16[384,320]{0,1:T(8,128)(2,1)S(1)} %collective-permute-done.3), channel_id=1, source_target_pairs={{0,1},{1,2},{2,3},{3,4},{4,5},{5,6},{6,7},{7,0},{8,9},{9,10},{10,1... | collective-permute-start | bytes 737288 | tf_op jit(solution)/shard_map/ppermute | solution.py:57
  66.4 6.5 %collective-permute-start.5 = (bf16[384,320]{0,1:T(8,128)(2,1)S(1)}, bf16[384,320]{0,1:T(8,128)(2,1)S(1)}, u32[]{:S(2)}, u32[]{:S(2)}) collective-permute-start(bf16[384,320]{0,1:T(8,128)(2,1)S(1)} %collective-permute-done.4), channel_id=1, source_target_pairs={{0,1},{1,2},{2,3},{3,4},{4,5},{5,6},{6,7},{7,0},{8,9},{9,10},{10,1... | collective-permute-start | bytes 737288 | tf_op jit(solution)/shard_map/ppermute | solution.py:57
  72.9 6.5 %collective-permute-start.6 = (bf16[384,320]{0,1:T(8,128)(2,1)S(1)}, bf16[384,320]{0,1:T(8,128)(2,1)S(1)}, u32[]{:S(2)}, u32[]{:S(2)}) collective-permute-start(bf16[384,320]{0,1:T(8,128)(2,1)S(1)} %collective-permute-done.5), channel_id=1, source_target_pairs={{0,1},{1,2},{2,3},{3,4},{4,5},{5,6},{6,7},{7,0},{8,9},{9,10},{10,1... | collective-permute-start | bytes 737288 | tf_op jit(solution)/shard_map/ppermute | solution.py:57
  91.7 9.4 %copy-start.4 = (bf16[3072,320]{0,1:T(8,128)(2,1)S(1)}, bf16[3072,320]{0,1:T(8,128)(2,1)}, u32[]{:S(2)}) copy-start(bf16[3072,320]{0,1:T(8,128)(2,1)} %all-gather.2.cloned.1.call-done) | copy-start | bytes 5898244
  108.5 12.4 %copy-start.5 = (f32[320,2048]{1,0:T(8,128)}, f32[320,2048]{1,0:T(8,128)S(1)}, u32[]{:S(2)}) copy-start(f32[320,2048]{1,0:T(8,128)S(1)} %fusion.6) | copy-start | bytes 7864324
  149.3 50.5 %copy-start.1 = (bf16[384,128]{1,0:T(8,128)(2,1)S(1)}, bf16[384,128]{1,0:T(8,128)(2,1)}, u32[]{:S(2)}) copy-start(bf16[384,128]{1,0:T(8,128)(2,1)} %param.8) | copy-start | bytes 294916
  182.3 15.6 %copy-start.3 = (f32[128,2]{0,1:T(2,128)S(1)}, f32[128,2]{0,1:T(2,128)}, u32[]{:S(2)}) copy-start(f32[128,2]{0,1:T(2,128)} %param.10) | copy-start | bytes 3076
Sparse Core Ops, SparseCore 0:
  36.2 30.0 all-gather.1
